TPU v7x, 768 devices: a whole 4x8x12 slice. The times are simulated.
768 devices in a mesh: rows: 48 (over x, z), inner: 16 (over y, core).
Axes of the slice: x: 4, y: 8, z: 12, core: 2. Of those that a mesh axis runs over, the one named last changes fastest.
Arguments:
- factor: bfloat16 [96, 16, 128, 128], P('rows'), may hold values from -1.1953125 to 1.1953125
- target_blocks: bfloat16 [96, 16, 128, 128], P('rows', 'inner'), may hold values from -6 to 6
- diag_inverse: bfloat16 [96, 128, 128], P('rows'), may hold values from -0.5 to 0.5
- cols: int32 [96, 16], P('rows'), may hold values from -1 to 94, as said below
- pair_list: int32 [3, 48, 16, 16, 2], P(None, 'rows', 'inner'), may hold values from 0 to 15, as said below
Outputs:
- new_factor: bfloat16 [96, 16, 128, 128], P('rows', 'inner')
Inputs may be any that keep to these rules, and one draw needn't show every extreme that they name: cols[i, b] lies in i - 16 to i - 1 and is not below -1; only row 0 holds -1. `pair_list`: field 0 lies in 0 to 1, field 1 in 0 to 15, field 2 is 0 or 1; slots with flag 0 carry no pair.
All inputs are finite; a program needn't handle non-finite values.
Results may differ from a plain program's by a relative error of at most 0.014.
Values may be sent and summed in bfloat16 or wider, within the bound.
A program may use at most 32 MiB of HBM per device.

v0:
```python
import jax
import jax.numpy as jnp
from jax import lax
from jax.sharding import PartitionSpec as P

BAND = 16


def shifted(value, axis, steps):
    count = lax.axis_size(axis)
    first, last = (max(0, -steps), min(count, count - steps))
    return lax.ppermute(value, axis, [(source, source + steps) for source in range(first, last)])


def per_device(factor, target_blocks, diag_inverse, cols, pair_list):
    rows_here = factor.shape[0]
    own_slot = lax.axis_index("inner")
    row_group = lax.axis_index("rows")
    own_blocks = lax.dynamic_index_in_dim(factor, own_slot, 1, keepdims=False)
    hop_count = BAND // rows_here
    pieces = []
    for hop_index in range(hop_count, 0, -1):
        pieces.append(shifted((own_blocks, diag_inverse), "rows", hop_index))
    pieces.append((own_blocks, diag_inverse))
    window_factor = jnp.concatenate([piece[0] for piece in pieces], 0)
    window_inverse = jnp.concatenate([piece[1] for piece in pieces], 0)
    first_row = row_group * rows_here - BAND
    row_local = pair_list[0, 0, 0]
    left_slot = pair_list[1, 0, 0]
    live_flag = pair_list[2, 0, 0]
    slot_ids = jnp.arange(factor.shape[1], dtype=jnp.int32)
    columns = cols[row_local, slot_ids[:, None]]
    left_blocks = factor[row_local, left_slot]
    right_blocks = window_factor[columns - first_row]
    products = jnp.einsum(
        "bsxk,bsyk->bsxy", left_blocks, right_blocks, preferred_element_type=jnp.float32
    )
    group_rows = jnp.arange(rows_here, dtype=jnp.int32)
    row_tags = jnp.where(live_flag == 1, row_local, -1)
    arrived, arrived_tags = (
        lax.all_to_all(products, "inner", split_axis=0, concat_axis=1, tiled=True),
        lax.all_to_all(row_tags, "inner", split_axis=0, concat_axis=1, tiled=True),
    )
    weights = (arrived_tags[0][:, None] == group_rows).astype(jnp.float32)
    own_sums = jnp.einsum("ni,nxy->ixy", weights, arrived[0])
    difference = (target_blocks[:, 0].astype(jnp.float32) - own_sums).astype(jnp.bfloat16)
    own_cols = lax.dynamic_index_in_dim(cols, own_slot, 1, keepdims=False)
    inverses = window_inverse[own_cols - first_row]
    result = jnp.einsum("ixk,iky->ixy", difference, inverses, preferred_element_type=jnp.float32)
    return result.astype(jnp.bfloat16)[:, None]


def solution(mesh):
    placed = (
        P("rows", None, None, None),
        P("rows", "inner", None, None),
        P("rows", None, None),
        P("rows", None),
        P(None, "rows", "inner", None, None),
    )
    return jax.shard_map(
        per_device,
        mesh=mesh,
        in_specs=placed,
        out_specs=P("rows", "inner", None, None),
        check_vma=False,
    )
```

profile of v0, /device:TPU:11, one launch (start us, length us, event | category | flops | bytes accessed | tf_op | source)
XLA Modules:
  0.0 117.7 jit_solution(16259031999690266632)
XLA Ops:
  0.0 0.9 dynamic-slice_bitcast_fusion
  0.9 14.3 %collective-permute-start = (bf16[2,128,128]{2,1,0:T(8,128)(2,1)S(1)}, bf16[2,128,128]{2,1,0:T(8,128)(2,1)S(1)}, u32[]{:S(2)}, u32[]{:S(2)}) collective-permute-start(bf16[2,128,128]{2,1,0:T(8,128)(2,1)S(1)} %dynamic-slice_bitcast_fusion), channel_id=1, source_target_pairs={{0,128},{16,144},{32,160},{48,176},{64,192},{80,208},{96,224},{112... | collective-permute-start | bytes 196616 | tf_op jit(solution)/shard_map/ppermute | solution.py:12
  15.1 3.1 %collective-permute-start.1 = (bf16[2,128,128]{2,1,0:T(8,128)(2,1)S(1)}, bf16[2,128,128]{2,1,0:T(8,128)(2,1)S(1)}, u32[]{:S(2)}, u32[]{:S(2)}) collective-permute-start(bf16[2,128,128]{2,1,0:T(8,128)(2,1)S(1)} %dynamic-slice_bitcast_fusion), channel_id=1, source_target_pairs={{0,112},{16,128},{32,144},{48,160},{64,176},{80,192},{96,208},{112... | collective-permute-start | bytes 196616 | tf_op jit(solution)/shard_map/ppermute | solution.py:12
  18.3 9.4 %collective-permute-start.2 = (bf16[2,128,128]{2,1,0:T(8,128)(2,1)S(1)}, bf16[2,128,128]{2,1,0:T(8,128)(2,1)S(1)}, u32[]{:S(2)}, u32[]{:S(2)}) collective-permute-start(bf16[2,128,128]{2,1,0:T(8,128)(2,1)S(1)} %dynamic-slice_bitcast_fusion), channel_id=1, source_target_pairs={{0,96},{16,112},{32,128},{48,144},{64,160},{80,176},{96,192},{112,... | collective-permute-start | bytes 196616 | tf_op jit(solution)/shard_map/ppermute | solution.py:12
  27.7 1.9 %collective-permute-start.3 = (bf16[2,128,128]{2,1,0:T(8,128)(2,1)S(1)}, bf16[2,128,128]{2,1,0:T(8,128)(2,1)S(1)}, u32[]{:S(2)}, u32[]{:S(2)}) collective-permute-start(bf16[2,128,128]{2,1,0:T(8,128)(2,1)S(1)} %dynamic-slice_bitcast_fusion), channel_id=1, source_target_pairs={{0,80},{16,96},{32,112},{48,128},{64,144},{80,160},{96,176},{112,1... | collective-permute-start | bytes 196616 | tf_op jit(solution)/shard_map/ppermute | solution.py:12
  29.6 6.4 %collective-permute-start.4 = (bf16[2,128,128]{2,1,0:T(8,128)(2,1)S(1)}, bf16[2,128,128]{2,1,0:T(8,128)(2,1)S(1)}, u32[]{:S(2)}, u32[]{:S(2)}) collective-permute-start(bf16[2,128,128]{2,1,0:T(8,128)(2,1)S(1)} %dynamic-slice_bitcast_fusion), channel_id=1, source_target_pairs={{0,64},{16,80},{32,96},{48,112},{64,128},{80,144},{96,160},{112,17... | collective-permute-start | bytes 196616 | tf_op jit(solution)/shard_map/ppermute | solution.py:12
  36.0 0.0 copy-done.3
  36.0 0.7 copy.23
  36.7 9.3 %all-to-all-start = ((s32[16,1,2]{2,1,0:T(1,128)}), s32[16,1,2]{2,1,0:T(1,128)S(1)}, u32[]{:S(2)}, u32[]{:S(2)}) async-start(s32[16,1,2]{2,1,0:T(1,128)} %copy.23), calls=%async_computation | async-start | bytes 16384 | tf_op jit(solution)/shard_map/all_to_all | solution.py:42
  46.0 0.1 copy.25
  46.1 0.1 reshape.121
  46.2 0.0 copy-start
  46.2 0.7 copy-done
  46.8 0.8 gather_fusion.1
  47.6 0.1 sub.32
  47.7 0.1 copy.26
  47.8 0.1 copy.29
  47.9 0.1 reshape.129
  48.0 0.1 copy.24
  48.0 0.1 reshape.115
  48.1 0.0 copy-done.1
  48.2 0.8 gather_fusion
  48.9 0.0 collective-permute-done
  49.0 6.1 %collective-permute-start.5 = (bf16[2,128,128]{2,1,0:T(8,128)(2,1)S(1)}, bf16[2,128,128]{2,1,0:T(8,128)(2,1)S(1)}, u32[]{:S(2)}, u32[]{:S(2)}) collective-permute-start(bf16[2,128,128]{2,1,0:T(8,128)(2,1)S(1)} %dynamic-slice_bitcast_fusion), channel_id=1, source_target_pairs={{0,48},{16,64},{32,80},{48,96},{64,112},{80,128},{96,144},{112,160... | collective-permute-start | bytes 196616 | tf_op jit(solution)/shard_map/ppermute | solution.py:12
  55.1 0.0 collective-permute-done.1
  55.1 4.0 %collective-permute-start.6 = (bf16[2,128,128]{2,1,0:T(8,128)(2,1)S(1)}, bf16[2,128,128]{2,1,0:T(8,128)(2,1)S(1)}, u32[]{:S(2)}, u32[]{:S(2)}) collective-permute-start(bf16[2,128,128]{2,1,0:T(8,128)(2,1)S(1)} %dynamic-slice_bitcast_fusion), channel_id=1, source_target_pairs={{0,32},{16,48},{32,64},{48,80},{64,96},{80,112},{96,128},{112,144}... | collective-permute-start | bytes 196616 | tf_op jit(solution)/shard_map/ppermute | solution.py:12
  59.2 0.0 collective-permute-done.2
  59.2 1.9 %collective-permute-start.7 = (bf16[2,128,128]{2,1,0:T(8,128)(2,1)S(1)}, bf16[2,128,128]{2,1,0:T(8,128)(2,1)S(1)}, u32[]{:S(2)}, u32[]{:S(2)}) collective-permute-start(bf16[2,128,128]{2,1,0:T(8,128)(2,1)S(1)} %dynamic-slice_bitcast_fusion), channel_id=1, source_target_pairs={{0,16},{16,32},{32,48},{48,64},{64,80},{80,96},{96,112},{112,128},... | collective-permute-start | bytes 196616 | tf_op jit(solution)/shard_map/ppermute | solution.py:12
  61.1 0.0 collective-permute-done.3
  61.1 0.0 collective-permute-done.4
  61.2 0.2 collective-permute-done.5
  61.4 1.9 %collective-permute-done.6 = bf16[2,128,128]{2,1,0:T(8,128)(2,1)S(1)} collective-permute-done((bf16[2,128,128]{2,1,0:T(8,128)(2,1)S(1)}, bf16[2,128,128]{2,1,0:T(8,128)(2,1)S(1)}, u32[]{:S(2)}, u32[]{:S(2)}) %collective-permute-start.6) | collective-permute-done | bytes 65568 | tf_op jit(solution)/shard_map/ppermute | solution.py:12
  63.3 3.0 %collective-permute-done.7 = bf16[2,128,128]{2,1,0:T(8,128)(2,1)S(1)} collective-permute-done((bf16[2,128,128]{2,1,0:T(8,128)(2,1)S(1)}, bf16[2,128,128]{2,1,0:T(8,128)(2,1)S(1)}, u32[]{:S(2)}, u32[]{:S(2)}) %collective-permute-start.7) | collective-permute-done | bytes 65568 | tf_op jit(solution)/shard_map/ppermute | solution.py:12
  66.3 0.7 gather_fusion.2
  67.1 1.8 %fusion.21 = bf16[16,2,128,128]{3,2,1,0:T(8,128)(2,1)} fusion(bf16[16,2,128,128]{3,2,1,0:T(8,128)(2,1)S(1)} %bitcast.36, bf16[16,2,128,128]{3,2,1,0:T(8,128)(2,1)S(1)} %bitcast.37), kind=kOutput, calls=%fused_computation.50 | convolution fusion | flops 134217728 | bytes 3145728 | tf_op jit(solution)/shard_map/bsxk,bsyk->bsxy/dot_general | solution.py:35
  68.9 0.0 all-to-all-done
  68.9 9.1 %all-to-all-start.1 = ((bf16[16,2,128,128]{3,2,1,0:T(8,128)(2,1)}), bf16[16,2,128,128]{3,2,1,0:T(8,128)(2,1)S(1)}, u32[]{:S(2)}, u32[]{:S(2)}) async-start(bf16[16,2,128,128]{3,2,1,0:T(8,128)(2,1)} %fusion.21), calls=%async_computation.1 | async-start | bytes 2097152 | tf_op jit(solution)/shard_map/all_to_all | solution.py:41
  78.0 0.0 copy-done.2
  78.0 1.9 %collective-permute-start.8 = (bf16[2,128,128]{2,1,0:T(8,128)(2,1)S(1)}, bf16[2,128,128]{2,1,0:T(8,128)(2,1)S(1)}, u32[]{:S(2)}, u32[]{:S(2)}) collective-permute-start(bf16[2,128,128]{2,1,0:T(8,128)(2,1)S(1)} %copy-done.2), channel_id=1, source_target_pairs={{0,128},{16,144},{32,160},{48,176},{64,192},{80,208},{96,224},{112... | collective-permute-start | bytes 196616 | tf_op jit(solution)/shard_map/ppermute | solution.py:12
  79.9 1.9 %collective-permute-start.9 = (bf16[2,128,128]{2,1,0:T(8,128)(2,1)S(1)}, bf16[2,128,128]{2,1,0:T(8,128)(2,1)S(1)}, u32[]{:S(2)}, u32[]{:S(2)}) collective-permute-start(bf16[2,128,128]{2,1,0:T(8,128)(2,1)S(1)} %copy-done.2), channel_id=1, source_target_pairs={{0,112},{16,128},{32,144},{48,160},{64,176},{80,192},{96,208},{112... | collective-permute-start | bytes 196616 | tf_op jit(solution)/shard_map/ppermute | solution.py:12
  81.9 4.0 %collective-permute-start.10 = (bf16[2,128,128]{2,1,0:T(8,128)(2,1)S(1)}, bf16[2,128,128]{2,1,0:T(8,128)(2,1)S(1)}, u32[]{:S(2)}, u32[]{:S(2)}) collective-permute-start(bf16[2,128,128]{2,1,0:T(8,128)(2,1)S(1)} %copy-done.2), channel_id=1, source_target_pairs={{0,96},{16,112},{32,128},{48,144},{64,160},{80,176},{96,192},{112,... | collective-permute-start | bytes 196616 | tf_op jit(solution)/shard_map/ppermute | solution.py:12
  85.8 1.9 %collective-permute-start.11 = (bf16[2,128,128]{2,1,0:T(8,128)(2,1)S(1)}, bf16[2,128,128]{2,1,0:T(8,128)(2,1)S(1)}, u32[]{:S(2)}, u32[]{:S(2)}) collective-permute-start(bf16[2,128,128]{2,1,0:T(8,128)(2,1)S(1)} %copy-done.2), channel_id=1, source_target_pairs={{0,80},{16,96},{32,112},{48,128},{64,144},{80,160},{96,176},{112,1... | collective-permute-start | bytes 196616 | tf_op jit(solution)/shard_map/ppermute | solution.py:12
  87.8 1.9 %collective-permute-start.12 = (bf16[2,128,128]{2,1,0:T(8,128)(2,1)S(1)}, bf16[2,128,128]{2,1,0:T(8,128)(2,1)S(1)}, u32[]{:S(2)}, u32[]{:S(2)}) collective-permute-start(bf16[2,128,128]{2,1,0:T(8,128)(2,1)S(1)} %copy-done.2), channel_id=1, source_target_pairs={{0,64},{16,80},{32,96},{48,112},{64,128},{80,144},{96,160},{112,17... | collective-permute-start | bytes 196616 | tf_op jit(solution)/shard_map/ppermute | solution.py:12
  89.7 0.2 fusion.18
  89.9 0.5 broadcast.157
  90.4 0.7 reduce.5
  91.1 0.1 eq.31
  91.2 4.0 %collective-permute-done.8 = bf16[2,128,128]{2,1,0:T(8,128)(2,1)S(1)} collective-permute-done((bf16[2,128,128]{2,1,0:T(8,128)(2,1)S(1)}, bf16[2,128,128]{2,1,0:T(8,128)(2,1)S(1)}, u32[]{:S(2)}, u32[]{:S(2)}) %collective-permute-start.8) | collective-permute-done | bytes 65568 | tf_op jit(solution)/shard_map/ppermute | solution.py:12
  95.2 1.9 %collective-permute-start.13 = (bf16[2,128,128]{2,1,0:T(8,128)(2,1)S(1)}, bf16[2,128,128]{2,1,0:T(8,128)(2,1)S(1)}, u32[]{:S(2)}, u32[]{:S(2)}) collective-permute-start(bf16[2,128,128]{2,1,0:T(8,128)(2,1)S(1)} %copy-done.2), channel_id=1, source_target_pairs={{0,48},{16,64},{32,80},{48,96},{64,112},{80,128},{96,144},{112,160... | collective-permute-start | bytes 196616 | tf_op jit(solution)/shard_map/ppermute | solution.py:12
  97.1 0.0 collective-permute-done.9
  97.1 4.4 %collective-permute-start.14 = (bf16[2,128,128]{2,1,0:T(8,128)(2,1)S(1)}, bf16[2,128,128]{2,1,0:T(8,128)(2,1)S(1)}, u32[]{:S(2)}, u32[]{:S(2)}) collective-permute-start(bf16[2,128,128]{2,1,0:T(8,128)(2,1)S(1)} %copy-done.2), channel_id=1, source_target_pairs={{0,32},{16,48},{32,64},{48,80},{64,96},{80,112},{96,128},{112,144}... | collective-permute-start | bytes 196616 | tf_op jit(solution)/shard_map/ppermute | solution.py:12
  101.5 0.0 collective-permute-done.10
  101.6 4.0 %collective-permute-start.15 = (bf16[2,128,128]{2,1,0:T(8,128)(2,1)S(1)}, bf16[2,128,128]{2,1,0:T(8,128)(2,1)S(1)}, u32[]{:S(2)}, u32[]{:S(2)}) collective-permute-start(bf16[2,128,128]{2,1,0:T(8,128)(2,1)S(1)} %copy-done.2), channel_id=1, source_target_pairs={{0,16},{16,32},{32,48},{48,64},{64,80},{80,96},{96,112},{112,128},... | collective-permute-start | bytes 196616 | tf_op jit(solution)/shard_map/ppermute | solution.py:12
  105.6 0.7 collective-permute-done.11
  106.4 0.0 collective-permute-done.12
  106.4 6.8 %collective-permute-done.13 = bf16[2,128,128]{2,1,0:T(8,128)(2,1)S(1)} collective-permute-done((bf16[2,128,128]{2,1,0:T(8,128)(2,1)S(1)}, bf16[2,128,128]{2,1,0:T(8,128)(2,1)S(1)}, u32[]{:S(2)}, u32[]{:S(2)}) %collective-permute-start.13) | collective-permute-done | bytes 65568 | tf_op jit(solution)/shard_map/ppermute | solution.py:12
  113.2 0.0 collective-permute-done.14
  113.2 2.1 %collective-permute-done.15 = bf16[2,128,128]{2,1,0:T(8,128)(2,1)S(1)} collective-permute-done((bf16[2,128,128]{2,1,0:T(8,128)(2,1)S(1)}, bf16[2,128,128]{2,1,0:T(8,128)(2,1)S(1)}, u32[]{:S(2)}, u32[]{:S(2)}) %collective-permute-start.15) | collective-permute-done | bytes 65568 | tf_op jit(solution)/shard_map/ppermute | solution.py:12
  115.4 0.0 copy-start.4
  115.4 0.6 gather_fusion.3
  116.0 0.0 all-to-all-done.1
  116.0 0.3 copy-done.4
  116.2 0.7 fusion.5
  116.9 0.8 fusion.8
  (27 shorter events, 0.3 us)
Async XLA Ops:
  0.0 36.0 %copy-start.3 = (s32[3,1,1,16,2]{3,4,2,1,0:T(2,128)S(1)}, s32[3,1,1,16,2]{3,4,2,1,0:T(2,128)}, u32[]{:S(2)}) copy-start(s32[3,1,1,16,2]{3,4,2,1,0:T(2,128)} %param.9) | copy-start | bytes 1156
  0.9 48.1 %collective-permute-start = (bf16[2,128,128]{2,1,0:T(8,128)(2,1)S(1)}, bf16[2,128,128]{2,1,0:T(8,128)(2,1)S(1)}, u32[]{:S(2)}, u32[]{:S(2)}) collective-permute-start(bf16[2,128,128]{2,1,0:T(8,128)(2,1)S(1)} %dynamic-slice_bitcast_fusion), channel_id=1, source_target_pairs={{0,128},{16,144},{32,160},{48,176},{64,192},{80,208},{96,224},{112... | collective-permute-start | bytes 196616 | tf_op jit(solution)/shard_map/ppermute | solution.py:12
  15.1 40.0 %collective-permute-start.1 = (bf16[2,128,128]{2,1,0:T(8,128)(2,1)S(1)}, bf16[2,128,128]{2,1,0:T(8,128)(2,1)S(1)}, u32[]{:S(2)}, u32[]{:S(2)}) collective-permute-start(bf16[2,128,128]{2,1,0:T(8,128)(2,1)S(1)} %dynamic-slice_bitcast_fusion), channel_id=1, source_target_pairs={{0,112},{16,128},{32,144},{48,160},{64,176},{80,192},{96,208},{112... | collective-permute-start | bytes 196616 | tf_op jit(solution)/shard_map/ppermute | solution.py:12
  18.3 40.9 %collective-permute-start.2 = (bf16[2,128,128]{2,1,0:T(8,128)(2,1)S(1)}, bf16[2,128,128]{2,1,0:T(8,128)(2,1)S(1)}, u32[]{:S(2)}, u32[]{:S(2)}) collective-permute-start(bf16[2,128,128]{2,1,0:T(8,128)(2,1)S(1)} %dynamic-slice_bitcast_fusion), channel_id=1, source_target_pairs={{0,96},{16,112},{32,128},{48,144},{64,160},{80,176},{96,192},{112,... | collective-permute-start | bytes 196616 | tf_op jit(solution)/shard_map/ppermute | solution.py:12
  27.7 33.4 %collective-permute-start.3 = (bf16[2,128,128]{2,1,0:T(8,128)(2,1)S(1)}, bf16[2,128,128]{2,1,0:T(8,128)(2,1)S(1)}, u32[]{:S(2)}, u32[]{:S(2)}) collective-permute-start(bf16[2,128,128]{2,1,0:T(8,128)(2,1)S(1)} %dynamic-slice_bitcast_fusion), channel_id=1, source_target_pairs={{0,80},{16,96},{32,112},{48,128},{64,144},{80,160},{96,176},{112,1... | collective-permute-start | bytes 196616 | tf_op jit(solution)/shard_map/ppermute | solution.py:12
  29.6 31.5 %collective-permute-start.4 = (bf16[2,128,128]{2,1,0:T(8,128)(2,1)S(1)}, bf16[2,128,128]{2,1,0:T(8,128)(2,1)S(1)}, u32[]{:S(2)}, u32[]{:S(2)}) collective-permute-start(bf16[2,128,128]{2,1,0:T(8,128)(2,1)S(1)} %dynamic-slice_bitcast_fusion), channel_id=1, source_target_pairs={{0,64},{16,80},{32,96},{48,112},{64,128},{80,144},{96,160},{112,17... | collective-permute-start | bytes 196616 | tf_op jit(solution)/shard_map/ppermute | solution.py:12
  36.7 32.2 %all-to-all-start = ((s32[16,1,2]{2,1,0:T(1,128)}), s32[16,1,2]{2,1,0:T(1,128)S(1)}, u32[]{:S(2)}, u32[]{:S(2)}) async-start(s32[16,1,2]{2,1,0:T(1,128)} %copy.23), calls=%async_computation | async-start | bytes 16384 | tf_op jit(solution)/shard_map/all_to_all | solution.py:42
  46.2 0.7 copy-start
  46.8 1.3 %copy-start.1 = (bf16[2,16,128,128]{3,2,1,0:T(8,128)(2,1)S(1)}, bf16[2,16,128,128]{3,2,1,0:T(8,128)(2,1)}, u32[]{:S(2)}) copy-start(bf16[2,16,128,128]{3,2,1,0:T(8,128)(2,1)} %param.5) | copy-start | bytes 3145732
  49.0 12.4 %collective-permute-start.5 = (bf16[2,128,128]{2,1,0:T(8,128)(2,1)S(1)}, bf16[2,128,128]{2,1,0:T(8,128)(2,1)S(1)}, u32[]{:S(2)}, u32[]{:S(2)}) collective-permute-start(bf16[2,128,128]{2,1,0:T(8,128)(2,1)S(1)} %dynamic-slice_bitcast_fusion), channel_id=1, source_target_pairs={{0,48},{16,64},{32,80},{48,96},{64,112},{80,128},{96,144},{112,160... | collective-permute-start | bytes 196616 | tf_op jit(solution)/shard_map/ppermute | solution.py:12
  55.1 8.1 %collective-permute-start.6 = (bf16[2,128,128]{2,1,0:T(8,128)(2,1)S(1)}, bf16[2,128,128]{2,1,0:T(8,128)(2,1)S(1)}, u32[]{:S(2)}, u32[]{:S(2)}) collective-permute-start(bf16[2,128,128]{2,1,0:T(8,128)(2,1)S(1)} %dynamic-slice_bitcast_fusion), channel_id=1, source_target_pairs={{0,32},{16,48},{32,64},{48,80},{64,96},{80,112},{96,128},{112,144}... | collective-permute-start | bytes 196616 | tf_op jit(solution)/shard_map/ppermute | solution.py:12
  59.2 7.1 %collective-permute-start.7 = (bf16[2,128,128]{2,1,0:T(8,128)(2,1)S(1)}, bf16[2,128,128]{2,1,0:T(8,128)(2,1)S(1)}, u32[]{:S(2)}, u32[]{:S(2)}) collective-permute-start(bf16[2,128,128]{2,1,0:T(8,128)(2,1)S(1)} %dynamic-slice_bitcast_fusion), channel_id=1, source_target_pairs={{0,16},{16,32},{32,48},{48,64},{64,80},{80,96},{96,112},{112,128},... | collective-permute-start | bytes 196616 | tf_op jit(solution)/shard_map/ppermute | solution.py:12
  68.9 9.1 %copy-start.2 = (bf16[2,128,128]{2,1,0:T(8,128)(2,1)S(1)}, bf16[2,128,128]{2,1,0:T(8,128)(2,1)}, u32[]{:S(2)}) copy-start(bf16[2,128,128]{2,1,0:T(8,128)(2,1)} %param.7) | copy-start | bytes 196612
  68.9 47.0 %all-to-all-start.1 = ((bf16[16,2,128,128]{3,2,1,0:T(8,128)(2,1)}), bf16[16,2,128,128]{3,2,1,0:T(8,128)(2,1)S(1)}, u32[]{:S(2)}, u32[]{:S(2)}) async-start(bf16[16,2,128,128]{3,2,1,0:T(8,128)(2,1)} %fusion.21), calls=%async_computation.1 | async-start | bytes 2097152 | tf_op jit(solution)/shard_map/all_to_all | solution.py:41
  78.0 17.2 %collective-permute-start.8 = (bf16[2,128,128]{2,1,0:T(8,128)(2,1)S(1)}, bf16[2,128,128]{2,1,0:T(8,128)(2,1)S(1)}, u32[]{:S(2)}, u32[]{:S(2)}) collective-permute-start(bf16[2,128,128]{2,1,0:T(8,128)(2,1)S(1)} %copy-done.2), channel_id=1, source_target_pairs={{0,128},{16,144},{32,160},{48,176},{64,192},{80,208},{96,224},{112... | collective-permute-start | bytes 196616 | tf_op jit(solution)/shard_map/ppermute | solution.py:12
  79.9 17.2 %collective-permute-start.9 = (bf16[2,128,128]{2,1,0:T(8,128)(2,1)S(1)}, bf16[2,128,128]{2,1,0:T(8,128)(2,1)S(1)}, u32[]{:S(2)}, u32[]{:S(2)}) collective-permute-start(bf16[2,128,128]{2,1,0:T(8,128)(2,1)S(1)} %copy-done.2), channel_id=1, source_target_pairs={{0,112},{16,128},{32,144},{48,160},{64,176},{80,192},{96,208},{112... | collective-permute-start | bytes 196616 | tf_op jit(solution)/shard_map/ppermute | solution.py:12
  81.9 19.7 %collective-permute-start.10 = (bf16[2,128,128]{2,1,0:T(8,128)(2,1)S(1)}, bf16[2,128,128]{2,1,0:T(8,128)(2,1)S(1)}, u32[]{:S(2)}, u32[]{:S(2)}) collective-permute-start(bf16[2,128,128]{2,1,0:T(8,128)(2,1)S(1)} %copy-done.2), channel_id=1, source_target_pairs={{0,96},{16,112},{32,128},{48,144},{64,160},{80,176},{96,192},{112,... | collective-permute-start | bytes 196616 | tf_op jit(solution)/shard_map/ppermute | solution.py:12
  85.8 20.5 %collective-permute-start.11 = (bf16[2,128,128]{2,1,0:T(8,128)(2,1)S(1)}, bf16[2,128,128]{2,1,0:T(8,128)(2,1)S(1)}, u32[]{:S(2)}, u32[]{:S(2)}) collective-permute-start(bf16[2,128,128]{2,1,0:T(8,128)(2,1)S(1)} %copy-done.2), channel_id=1, source_target_pairs={{0,80},{16,96},{32,112},{48,128},{64,144},{80,160},{96,176},{112,1... | collective-permute-start | bytes 196616 | tf_op jit(solution)/shard_map/ppermute | solution.py:12
  87.8 18.6 %collective-permute-start.12 = (bf16[2,128,128]{2,1,0:T(8,128)(2,1)S(1)}, bf16[2,128,128]{2,1,0:T(8,128)(2,1)S(1)}, u32[]{:S(2)}, u32[]{:S(2)}) collective-permute-start(bf16[2,128,128]{2,1,0:T(8,128)(2,1)S(1)} %copy-done.2), channel_id=1, source_target_pairs={{0,64},{16,80},{32,96},{48,112},{64,128},{80,144},{96,160},{112,17... | collective-permute-start | bytes 196616 | tf_op jit(solution)/shard_map/ppermute | solution.py:12
  95.2 18.0 %collective-permute-start.13 = (bf16[2,128,128]{2,1,0:T(8,128)(2,1)S(1)}, bf16[2,128,128]{2,1,0:T(8,128)(2,1)S(1)}, u32[]{:S(2)}, u32[]{:S(2)}) collective-permute-start(bf16[2,128,128]{2,1,0:T(8,128)(2,1)S(1)} %copy-done.2), channel_id=1, source_target_pairs={{0,48},{16,64},{32,80},{48,96},{64,112},{80,128},{96,144},{112,160... | collective-permute-start | bytes 196616 | tf_op jit(solution)/shard_map/ppermute | solution.py:12
  97.1 16.0 %collective-permute-start.14 = (bf16[2,128,128]{2,1,0:T(8,128)(2,1)S(1)}, bf16[2,128,128]{2,1,0:T(8,128)(2,1)S(1)}, u32[]{:S(2)}, u32[]{:S(2)}) collective-permute-start(bf16[2,128,128]{2,1,0:T(8,128)(2,1)S(1)} %copy-done.2), channel_id=1, source_target_pairs={{0,32},{16,48},{32,64},{48,80},{64,96},{80,112},{96,128},{112,144}... | collective-permute-start | bytes 196616 | tf_op jit(solution)/shard_map/ppermute | solution.py:12
  101.6 13.8 %collective-permute-start.15 = (bf16[2,128,128]{2,1,0:T(8,128)(2,1)S(1)}, bf16[2,128,128]{2,1,0:T(8,128)(2,1)S(1)}, u32[]{:S(2)}, u32[]{:S(2)}) collective-permute-start(bf16[2,128,128]{2,1,0:T(8,128)(2,1)S(1)} %copy-done.2), channel_id=1, source_target_pairs={{0,16},{16,32},{32,48},{48,64},{64,80},{80,96},{96,112},{112,128},... | collective-permute-start | bytes 196616 | tf_op jit(solution)/shard_map/ppermute | solution.py:12
  115.4 0.8 copy-start.4
where the time goes:
time: 118 us
  starting transfers between devices  87.4 us (74%)
  waiting for transfers between devices  18.8 us (16%)
  local copies, waits for them, and re-layouts  6.86 us (6%)
  matrix products  3.3 us (3%)
    ppermute x16, starting transfers between devices, shifted(): lax.ppermute(value, axis, [(source, source + steps) for source in range(f...  69.1 us
    ppermute x16, waiting for transfers between devices, shifted(): lax.ppermute(value, axis, [(source, source + steps) for source in range(f...  18.8 us
    all_to_all x1, starting transfers between devices, per_device(): lax.all_to_all(row_tags, 'inner', split_axis=0, concat_axis=1, tiled=True)  9.28 us
    all_to_all x1, starting transfers between devices, per_device(): lax.all_to_all(products, 'inner', split_axis=0, concat_axis=1, tiled=True)  9.07 us
  transfers between devices with their start and end apart: 18, of which 7 were waited for; matrix products, arithmetic and copies ran while one was open for 7% of the time, Pallas kernels for 0%

commit v1 on v0

v1 whole, which is shorter than its diff:
```python
import jax
import jax.numpy as jnp
from jax import lax
from jax.experimental import pallas as pl
from jax.experimental.pallas import tpu as pltpu
from jax.sharding import PartitionSpec as P

MESH = pl.DeviceIdType.MESH
BAND = 16
BS = 128
GROUPS = 48
RING = 8
HOPS = 8
SLICE = 16
BLOCK = 2 * BS + 2 * SLICE
WINDOW = ((0, 2), (0, 8), (0, 1), (2, 4), (2, 3), (8, 7), (4, 5), (7, 6))
STEPS = tuple(sorted({m - k for k, m in WINDOW}))
EDGE_OF = {m: n for n, (k, m) in enumerate(WINDOW)}
ROUND = tuple(range(1, RING))
ORDER = (3, 5, 4, 1, 7, 2, 6, 0)


def kernel(
    factor, target, inverse, cols, pairs, out,
    left, own, mate, mate_pairs, part, far, inv_out, inv_in, near, goal,
    local_sem, win_send, win_recv, mate_send, mate_recv, list_send, list_recv,
    sum_send, sum_recv, inv_send, inv_recv,
):
    group = lax.axis_index("rows")
    slot = lax.axis_index("inner")
    ring_at = slot // 2
    core = slot % 2
    other = slot + 1 - 2 * core
    first_row = group * 2 - BAND

    def along(step):
        return (lax.rem(group + step + GROUPS, GROUPS), slot)

    def around(step):
        return (group, lax.rem(ring_at + step + RING, RING) * 2 + core)

    sibling = (group, other)

    loads = [
        pltpu.make_async_copy(factor.at[:, slot], own.at[0, :, pl.ds(0, BS)], local_sem.at[0]),
        pltpu.make_async_copy(
            inverse.at[:, pl.ds(pl.multiple_of(ring_at * SLICE, SLICE), SLICE)],
            own.at[0, :, pl.ds(BS, SLICE)],
            local_sem.at[1],
        ),
        pltpu.make_async_copy(factor.at[:, other], mate.at[0], local_sem.at[2]),
        pltpu.make_async_copy(factor, left, local_sem.at[3]),
        pltpu.make_async_copy(target, goal, local_sem.at[4]),
    ]
    for load in loads:
        load.start()

    barrier = pltpu.get_barrier_semaphore()
    for step in STEPS:
        pl.semaphore_signal(barrier, inc=1, device_id=along(-step), device_id_type=MESH)
    for step in ROUND:
        pl.semaphore_signal(barrier, inc=1, device_id=around(-step), device_id_type=MESH)
    pl.semaphore_signal(barrier, inc=1, device_id=sibling, device_id_type=MESH)
    loads[0].wait()
    loads[1].wait()
    pl.semaphore_wait(barrier, len(STEPS) + len(ROUND) + 1)

    def remote(source, destination, send_sem, recv_sem, device):
        return pltpu.make_async_remote_copy(
            src_ref=source, dst_ref=destination, send_sem=send_sem, recv_sem=recv_sem,
            device_id=device, device_id_type=MESH,
        )

    sent = []

    def send(*where):
        copy = remote(*where)
        copy.start()
        sent.append(copy)

    def window_copy(n):
        k, m = WINDOW[n]
        return own.at[k], own.at[m], win_send.at[n], win_recv.at[n], along(m - k)

    def mate_copy(k):
        return own.at[k, :, pl.ds(0, BS)], mate.at[k], mate_send.at[k - 1], mate_recv.at[k - 1], sibling

    for n, (k, m) in enumerate(WINDOW):
        if k == 0:
            send(*window_copy(n))
    list_copy = (pairs, mate_pairs, list_send.at[0], list_recv.at[0], sibling)
    send(*list_copy)
    for arrival, (_, held) in enumerate(WINDOW):
        remote(*window_copy(arrival)).wait_recv()
        for n, (k, m) in enumerate(WINDOW):
            if k == held:
                send(*window_copy(n))
        send(*mate_copy(held))
    for load in loads[2:]:
        load.wait()
    remote(*list_copy).wait_recv()
    for _, held in WINDOW:
        remote(*mate_copy(held)).wait_recv()

    def locate(row, column):
        relative = cols[row, column] - first_row
        back = HOPS - lax.shift_right_arithmetic(relative, 1)
        return jnp.clip(back, 0, HOPS), relative & 1

    def partial_sums(e):
        column = lax.rem(ring_at + e, RING) * 2 + core
        totals = [jnp.zeros((BS, BS), jnp.float32) for _ in range(2)]
        for table, window in ((pairs, own), (mate_pairs, mate)):
            for s in range(2):
                row = table[0, 0, 0, s, column]
                a = table[1, 0, 0, s, column]
                live = table[2, 0, 0, s, column]
                back, half = locate(row, column)
                product = lax.dot_general(
                    left[row, a], window[back, half, pl.ds(0, BS)],
                    (((1,), (1,)), ((), ())), preferred_element_type=jnp.float32,
                )
                for i in range(2):
                    wanted = jnp.logical_and(live == 1, row == i)
                    totals[i] = totals[i] + jnp.where(wanted, product, 0.0)
        return totals

    def hold(e):
        for i, total in enumerate(partial_sums(e)):
            part[e, i] = total.astype(jnp.bfloat16)

    def sum_copy(n):
        source, destination, step = {
            0: (part.at[3], near.at[0], 1),
            1: (part.at[5], near.at[1], -1),
            2: (part.at[4, 0], far.at[0], -2),
            3: (part.at[4, 1], far.at[1], 2),
            4: (part.at[1], near.at[2], 1),
            5: (part.at[7], near.at[3], -1),
            6: (part.at[2], near.at[4], 2),
            7: (part.at[6], near.at[5], -2),
        }[n]
        return source, destination, sum_send.at[n], sum_recv.at[n], around(step)

    def inverse_copy(e):
        place = pl.ds(pl.multiple_of(ring_at * SLICE, SLICE), SLICE)
        return inv_out.at[e], inv_in.at[:, place], inv_send.at[e - 1], inv_recv.at[e - 1], around(e)

    hold(3)
    send(*sum_copy(0))
    hold(5)
    send(*sum_copy(1))
    hold(4)
    send(*sum_copy(2))
    send(*sum_copy(3))
    for e in (4, 3, 5, 2, 6, 1, 7, 0):
        column = lax.rem(ring_at + e, RING) * 2 + core
        for i in range(2):
            back, half = locate(i, column)
            inv_out[e, i] = own[back, half, pl.ds(BS, SLICE)]
        if e:
            send(*inverse_copy(e))
    hold(1)
    send(*sum_copy(4))
    hold(7)
    send(*sum_copy(5))
    for e, n, first, second, extra_row, extra in ((2, 6, 0, 3, 1, 1), (6, 7, 1, 2, 0, 0)):
        totals = partial_sums(e)
        remote(*sum_copy(first)).wait_recv()
        remote(*sum_copy(second)).wait_recv()
        for i in range(2):
            total = totals[i] + near[first, i].astype(jnp.float32)
            if i == extra_row:
                total = total + far[extra].astype(jnp.float32)
            part[e, i] = total.astype(jnp.bfloat16)
        send(*sum_copy(n))
    totals = partial_sums(0)
    inv_in[:, pl.ds(pl.multiple_of(ring_at * SLICE, SLICE), SLICE), :] = inv_out[0]
    for n in (4, 5, 6, 7):
        remote(*sum_copy(n)).wait_recv()
        for i in range(2):
            totals[i] = totals[i] + near[n - 2, i].astype(jnp.float32)
    for e in ROUND:
        place = pl.ds(pl.multiple_of(lax.rem(ring_at - e + RING, RING) * SLICE, SLICE), SLICE)
        remote(
            inv_out.at[e], inv_in.at[:, place], inv_send.at[e - 1], inv_recv.at[e - 1], around(e)
        ).wait_recv()
    for i in range(2):
        difference = (goal[i, 0].astype(jnp.float32) - totals[i]).astype(jnp.bfloat16)
        result = jnp.dot(difference, inv_in[i], preferred_element_type=jnp.float32)
        result = jnp.where(cols[i, slot] < 0, 0.0, result)
        out[i, 0] = result.astype(jnp.bfloat16)
    for copy in sent:
        copy.wait_send()


def per_device(factor, target_blocks, diag_inverse, cols, pair_list):
    bf16 = jnp.bfloat16
    anywhere = pl.BlockSpec(memory_space=pltpu.HBM)
    scalars = pl.BlockSpec(memory_space=pltpu.SMEM)
    dma = pltpu.SemaphoreType.DMA
    return pl.pallas_call(
        kernel,
        out_shape=jax.ShapeDtypeStruct((2, 1, BS, BS), bf16),
        in_specs=[anywhere, anywhere, anywhere, scalars, scalars],
        out_specs=pl.BlockSpec(memory_space=pltpu.VMEM),
        scratch_shapes=[
            pltpu.VMEM((2, 16, BS, BS), bf16),
            pltpu.VMEM((HOPS + 1, 2, BS + SLICE, BS), bf16),
            pltpu.VMEM((HOPS + 1, 2, BS, BS), bf16),
            pltpu.SMEM((3, 1, 1, 2, 16), jnp.int32),
            pltpu.VMEM((RING, 2, BS, BS), bf16),
            pltpu.VMEM((2, BS, BS), bf16),
            pltpu.VMEM((RING, 2, SLICE, BS), bf16),
            pltpu.VMEM((2, BS, BS), bf16),
            pltpu.VMEM((6, 2, BS, BS), bf16),
            pltpu.VMEM((2, 1, BS, BS), bf16),
            dma((5,)),
            dma((len(WINDOW),)),
            dma((len(WINDOW),)),
            dma((HOPS,)),
            dma((HOPS,)),
            dma((1,)),
            dma((1,)),
            dma((8,)),
            dma((8,)),
            dma((RING - 1,)),
            dma((RING - 1,)),
        ],
        compiler_params=pltpu.CompilerParams(
            collective_id=0, has_side_effects=True, vmem_limit_bytes=60 * 1024 * 1024
        ),
        name="sweep",
    )(factor, target_blocks, diag_inverse, cols, jnp.swapaxes(pair_list, 3, 4))


def solution(mesh):
    placed = (
        P("rows", None, None, None),
        P("rows", "inner", None, None),
        P("rows", None, None),
        P("rows", None),
        P(None, "rows", "inner", None, None),
    )
    return jax.shard_map(
        per_device,
        mesh=mesh,
        in_specs=placed,
        out_specs=P("rows", "inner", None, None),
        check_vma=False,
    )
```

time: 118 us -> 50.6 us (0.43)
  the two profiles are of different devices: /device:TPU:11 before, /device:TPU:1 now
where the time goes in v1:
time: 50.6 us; the launch traced here: 50.3 us
  Pallas kernels  48.9 us (97%)
  local copies, waits for them, and re-layouts  1.47 us (3%)
    pallas_call x1, Pallas kernels, per_device(): pl.pallas_call(kernel, out_shape=jax.ShapeDtypeStruct((2, 1, BS, BS), bf1...  48.9 us
    unnamed x1, local copies, waits for them, and re-layouts  1.47 us

profile of v1, /device:TPU:1, one launch (start us, length us, event | category | flops | bytes accessed | tf_op | source)
XLA Modules:
  0.0 50.3 jit_solution(4038493315690566666)
XLA Ops:
  0.0 48.9 %sweep.1 = bf16[2,1,128,128]{3,2,1,0:T(8,128)(2,1)} custom-call(bf16[2,16,128,128]{3,2,1,0:T(8,128)(2,1)} %factor.1, bf16[2,1,128,128]{3,2,1,0:T(8,128)(2,1)} %target.1, bf16[2,128,128]{2,1,0:T(8,128)(2,1)} %inverse.1, s32[2,16]{1,0:T(2,128)} %cols.1, s32[3,1,1,2,16]{4,3,2,1,0:T(2,128)} %bitcast.1), custom_call_target="tpu_custom_call" | custom-call | tf_op jit(solution)/shard_map/sweep/pallas_call | solution.py:202
  48.9 1.5 %copy.7 = bf16[2,1,128,128]{3,2,1,0:T(8,128)(2,1)} copy(bf16[2,1,128,128]{3,2,1,0:T(8,128)(2,1)} %sweep.1) | data formatting | bytes 131072

commit v2 on v1

v2 whole, which is shorter than its diff:
```python
import jax
import jax.numpy as jnp
from jax import lax
from jax.experimental import pallas as pl
from jax.experimental.pallas import tpu as pltpu
from jax.sharding import PartitionSpec as P

MESH = pl.DeviceIdType.MESH
BAND = 16
BS = 128
GROUPS = 48
RING = 8
HOPS = 8
SLICE = 16
WINDOW = ((0, 2), (0, 8), (0, 1), (2, 4), (2, 3), (8, 7), (4, 5), (7, 6))
ENDS = ((40, 0, 7), (41, 0, 6))
ARRIVALS = tuple((m, q) for stage in ((2, 8, 1), (4, 3, 7), (5, 6)) for q in range(3) for m in stage)
HALF = BS // 2
ROUND = tuple(range(1, RING))


def kernel(
    factor, target, inverse, cols_in, pairs_in, out,
    left, own, slab, mate, cols, pairs, mate_pairs, part, far, inv_out, inv_in, near, goal,
    local_sem, win_send, win_recv, end_send, mate_send, mate_recv, list_send, list_recv,
    sum_send, sum_recv, inv_send, inv_recv, greet,
):
    group = lax.axis_index("rows")
    slot = lax.axis_index("inner")
    ring_at = slot // 2
    core = slot % 2
    other = slot + 1 - 2 * core
    first_row = group * 2 - BAND
    my_slice = pl.ds(pl.multiple_of(ring_at * SLICE, SLICE), SLICE)

    def along(step):
        return (group + step, slot)

    def around(step):
        return (group, lax.rem(ring_at + step + RING, RING) * 2 + core)

    sibling = (group, other)

    loads = [
        pltpu.make_async_copy(factor.at[:, slot], own.at[0], local_sem.at[0]),
        pltpu.make_async_copy(inverse.at[:, my_slice], slab.at[0], local_sem.at[1]),
        pltpu.make_async_copy(cols_in, cols, local_sem.at[2]),
        pltpu.make_async_copy(pairs_in, pairs, local_sem.at[3]),
        pltpu.make_async_copy(factor.at[:, other], mate.at[0], local_sem.at[4]),
        pltpu.make_async_copy(target, goal, local_sem.at[5]),
        pltpu.make_async_copy(factor, left, local_sem.at[6]),
    ]

    def remote(source, destination, send_sem, recv_sem, device):
        return pltpu.make_async_remote_copy(
            src_ref=source, dst_ref=destination, send_sem=send_sem, recv_sem=recv_sem,
            device_id=device, device_id_type=MESH,
        )

    def active(k, m):
        return jnp.logical_and(group >= k, group - k + max(k, m) < GROUPS)

    steps = {}
    for k, m in WINDOW:
        d = m - k
        sends = active(k, m)
        comes = jnp.logical_and(group >= m, group - m + max(k, m) < GROUPS)
        if d in steps:
            sends = jnp.logical_or(sends, steps[d][0])
            comes = jnp.logical_or(comes, steps[d][1])
        steps[d] = (sends, comes)
    for g, k, m in ENDS:
        d = m - k
        sends, comes = group == g, group == g + d
        if d in steps:
            sends = jnp.logical_or(sends, steps[d][0])
            comes = jnp.logical_or(comes, steps[d][1])
        steps[d] = (sends, comes)

    barrier = pltpu.get_barrier_semaphore()
    for step in (1, -1):
        pl.semaphore_signal(barrier, inc=1, device_id=around(step), device_id_type=MESH)
    pl.semaphore_signal(barrier, inc=1, device_id=sibling, device_id_type=MESH)
    partners = jnp.int32(3)
    for d, (sends, comes) in steps.items():
        @pl.when(comes)
        def _():
            pl.semaphore_signal(barrier, inc=1, device_id=along(-d), device_id_type=MESH)
        partners = partners + sends.astype(jnp.int32)
    for load in loads:
        load.start()
    loads[0].wait()
    loads[1].wait()
    pl.semaphore_wait(barrier, partners)

    def piece(k, q):
        return slab.at[k] if q == 2 else own.at[k, :, pl.ds(q * HALF, HALF)]

    def window_copy(k, m, q, send_sem):
        return remote(piece(k, q), piece(m, q), send_sem, win_recv.at[m - 1, q], along(m - k))

    def mate_copy(k, q):
        place = pl.ds(q * HALF, HALF)
        return remote(
            own.at[k, :, place], mate.at[k, :, place],
            mate_send.at[k - 1, q], mate_recv.at[k - 1, q], sibling,
        )

    def pass_on(held, q):
        for n, (k, m) in enumerate(WINDOW):
            if k == held:
                @pl.when(active(k, m))
                def _():
                    window_copy(k, m, q, win_send.at[n, q]).start()
        for n, (g, k, m) in enumerate(ENDS):
            if k == held:
                @pl.when(group == g)
                def _():
                    window_copy(k, m, q, end_send.at[n, q]).start()
        if held and q < 2:
            mate_copy(held, q).start()

    list_copy = remote(pairs, mate_pairs, list_send.at[0], list_recv.at[0], sibling)

    def greeting(n):
        for way, step in enumerate((1, -1)):
            pl.semaphore_signal(greet.at[n, way], inc=1, device_id=around(step), device_id_type=MESH)

    def greeted(n):
        for way in range(2):
            pl.semaphore_wait(greet.at[n, way], 1)

    for q in range(3):
        pass_on(0, q)
    greeting(0)
    loads[3].wait()
    list_copy.start()

    def arrive(m, q):
        @pl.when(group >= m)
        def _():
            window_copy(0, m, q, win_send.at[0, q]).wait_recv()
            pass_on(m, q)

    def mates(q):
        for m in range(1, HOPS + 1):
            @pl.when(group >= m)
            def _():
                mate_copy(m, q).wait_recv()

    pending = list(ARRIVALS)

    def gather(upto):
        while pending:
            m, q = pending.pop(0)
            arrive(m, q)
            if (m, q) == upto:
                return

    for n in range(3):
        gather(ARRIVALS[3 * n + 2])
        greeted(n)
        if n < 2:
            greeting(n + 1)
    gather(None)
    for load in loads[2:3] + loads[4:]:
        load.wait()
    list_copy.wait_recv()
    for q in range(2):
        mates(q)

    def locate(row, column):
        relative = cols[row, column] - first_row
        back = HOPS - lax.shift_right_arithmetic(relative, 1)
        return jnp.clip(back, 0, HOPS), relative & 1

    def partial_sums(e):
        column = lax.rem(ring_at + e, RING) * 2 + core
        totals = [jnp.zeros((BS, BS), jnp.float32) for _ in range(2)]
        for table, window in ((pairs, own), (mate_pairs, mate)):
            for s in range(2):
                row = table[0, 0, 0, s, column]
                a = table[1, 0, 0, s, column]
                live = table[2, 0, 0, s, column]
                back, half = locate(row, column)
                product = lax.dot_general(
                    left[row, a], window[back, half],
                    (((1,), (1,)), ((), ())), preferred_element_type=jnp.float32,
                )
                for i in range(2):
                    wanted = jnp.logical_and(live == 1, row == i)
                    totals[i] = totals[i] + jnp.where(wanted, product, 0.0)
        return totals

    sent = []

    def hold(e):
        for i, total in enumerate(partial_sums(e)):
            part[e, i] = total.astype(jnp.bfloat16)

    def sum_copy(n):
        source, destination, step = {
            0: (part.at[3], near.at[0], 1),
            1: (part.at[5], near.at[1], -1),
            2: (part.at[4, 0], far.at[0], -2),
            3: (part.at[4, 1], far.at[1], 2),
            4: (part.at[1], near.at[2], 1),
            5: (part.at[7], near.at[3], -1),
            6: (part.at[2], near.at[4], 2),
            7: (part.at[6], near.at[5], -2),
        }[n]
        return remote(source, destination, sum_send.at[n], sum_recv.at[n], around(step))

    def inverse_copy(e, place):
        return remote(inv_out.at[e], inv_in.at[:, place], inv_send.at[e - 1], inv_recv.at[e - 1], around(e))

    def send(copy):
        copy.start()
        sent.append(copy)

    hold(3)
    send(sum_copy(0))
    hold(5)
    send(sum_copy(1))
    hold(4)
    send(sum_copy(2))
    send(sum_copy(3))
    for e in (4, 3, 5, 2, 6, 1, 7, 0):
        column = lax.rem(ring_at + e, RING) * 2 + core
        for i in range(2):
            back, half = locate(i, column)
            inv_out[e, i] = slab[back, half]
        if e:
            send(inverse_copy(e, my_slice))
    hold(1)
    send(sum_copy(4))
    hold(7)
    send(sum_copy(5))
    for e, n, first, second, extra in ((2, 6, 0, 3, 1), (6, 7, 1, 2, 0)):
        totals = partial_sums(e)
        sum_copy(first).wait_recv()
        sum_copy(second).wait_recv()
        for i in range(2):
            total = totals[i] + near[first, i].astype(jnp.float32)
            if i == extra:
                total = total + far[extra].astype(jnp.float32)
            part[e, i] = total.astype(jnp.bfloat16)
        send(sum_copy(n))
    totals = partial_sums(0)
    inv_in[:, my_slice, :] = inv_out[0]
    for n in (4, 5, 6, 7):
        sum_copy(n).wait_recv()
        for i in range(2):
            totals[i] = totals[i] + near[n - 2, i].astype(jnp.float32)
    for e in ROUND:
        start = lax.rem(ring_at - e + RING, RING) * SLICE
        inverse_copy(e, pl.ds(pl.multiple_of(start, SLICE), SLICE)).wait_recv()
    for i in range(2):
        difference = (goal[i, 0].astype(jnp.float32) - totals[i]).astype(jnp.bfloat16)
        result = jnp.dot(difference, inv_in[i], preferred_element_type=jnp.float32)
        result = jnp.where(cols[i, slot] < 0, 0.0, result)
        out[i, 0] = result.astype(jnp.bfloat16)
    for copy in sent:
        copy.wait_send()
    list_copy.wait_send()
    for q in range(3):
        for n, (k, m) in enumerate(WINDOW):
            @pl.when(active(k, m))
            def _():
                window_copy(k, m, q, win_send.at[n, q]).wait_send()
        for n, (g, k, m) in enumerate(ENDS):
            @pl.when(group == g)
            def _():
                window_copy(k, m, q, end_send.at[n, q]).wait_send()
        if q < 2:
            for m in range(1, HOPS + 1):
                @pl.when(group >= m)
                def _():
                    mate_copy(m, q).wait_send()


def per_device(factor, target_blocks, diag_inverse, cols, pair_list):
    bf16 = jnp.bfloat16
    anywhere = pl.BlockSpec(memory_space=pltpu.HBM)
    dma = pltpu.SemaphoreType.DMA
    return pl.pallas_call(
        kernel,
        out_shape=jax.ShapeDtypeStruct((2, 1, BS, BS), bf16),
        in_specs=[anywhere] * 5,
        out_specs=pl.BlockSpec(memory_space=pltpu.VMEM),
        scratch_shapes=[
            pltpu.VMEM((2, 16, BS, BS), bf16),
            pltpu.VMEM((HOPS + 1, 2, BS, BS), bf16),
            pltpu.VMEM((HOPS + 1, 2, SLICE, BS), bf16),
            pltpu.VMEM((HOPS + 1, 2, BS, BS), bf16),
            pltpu.SMEM((2, 16), jnp.int32),
            pltpu.SMEM((3, 1, 1, 2, 16), jnp.int32),
            pltpu.SMEM((3, 1, 1, 2, 16), jnp.int32),
            pltpu.VMEM((RING, 2, BS, BS), bf16),
            pltpu.VMEM((2, BS, BS), bf16),
            pltpu.VMEM((RING, 2, SLICE, BS), bf16),
            pltpu.VMEM((2, BS, BS), bf16),
            pltpu.VMEM((6, 2, BS, BS), bf16),
            pltpu.VMEM((2, 1, BS, BS), bf16),
            dma((7,)),
            dma((len(WINDOW), 3)),
            dma((HOPS, 3)),
            dma((len(ENDS), 3)),
            dma((HOPS, 2)),
            dma((HOPS, 2)),
            dma((1,)),
            dma((1,)),
            dma((8,)),
            dma((8,)),
            dma((RING - 1,)),
            dma((RING - 1,)),
            pltpu.SemaphoreType.REGULAR((3, 2)),
        ],
        compiler_params=pltpu.CompilerParams(
            collective_id=0, has_side_effects=True, vmem_limit_bytes=60 * 1024 * 1024
        ),
        name="sweep",
    )(factor, target_blocks, diag_inverse, cols, jnp.swapaxes(pair_list, 3, 4))


def solution(mesh):
    placed = (
        P("rows", None, None, None),
        P("rows", "inner", None, None),
        P("rows", None, None),
        P("rows", None),
        P(None, "rows", "inner", None, None),
    )
    return jax.shard_map(
        per_device,
        mesh=mesh,
        in_specs=placed,
        out_specs=P("rows", "inner", None, None),
        check_vma=False,
    )
```

time: 50.6 us -> 50.4 us (level)
  the two profiles are of different devices: /device:TPU:1 before, /device:TPU:6 now
where the time goes in v2:
time: 50.4 us; the launch traced here: 50.2 us
  Pallas kernels  48.7 us (97%)
  local copies, waits for them, and re-layouts  1.47 us (3%)
    pallas_call x1, Pallas kernels, per_device(): pl.pallas_call(kernel, out_shape=jax.ShapeDtypeStruct((2, 1, BS, BS), bf1...  48.7 us
    unnamed x1, local copies, waits for them, and re-layouts  1.47 us

profile of v2, /device:TPU:6, one launch (start us, length us, event | category | flops | bytes accessed | tf_op | source)
XLA Modules:
  0.0 50.2 jit_solution(17347370299061516672)
XLA Ops:
  0.0 48.7 %sweep.1 = bf16[2,1,128,128]{3,2,1,0:T(8,128)(2,1)} custom-call(bf16[2,16,128,128]{3,2,1,0:T(8,128)(2,1)} %factor.1, bf16[2,1,128,128]{3,2,1,0:T(8,128)(2,1)} %target.1, bf16[2,128,128]{2,1,0:T(8,128)(2,1)} %inverse.1, s32[2,16]{1,0:T(2,128)} %cols_in.1, s32[3,1,1,2,16]{4,3,2,1,0:T(2,128)} %bitcast.1), custom_call_target="tpu_custom_call" | custom-call | tf_op jit(solution)/shard_map/sweep/pallas_call | solution.py:286
  48.7 1.5 %copy.7 = bf16[2,1,128,128]{3,2,1,0:T(8,128)(2,1)} copy(bf16[2,1,128,128]{3,2,1,0:T(8,128)(2,1)} %sweep.1) | data formatting | bytes 131072

commit v3 on v2

v3 whole, which is shorter than its diff:
```python
import jax
import jax.numpy as jnp
from jax import lax
from jax.experimental import pallas as pl
from jax.experimental.pallas import tpu as pltpu
from jax.sharding import PartitionSpec as P

MESH = pl.DeviceIdType.MESH
BAND = 16
BS = 128
GROUPS = 48
RING = 8
HOPS = 8
SLICE = 16
WINDOW = ((0, 2), (0, 8), (0, 1), (2, 4), (2, 3), (8, 7), (4, 5), (7, 6))
ENDS = ((40, 4, 6), (41, 4, 6), (40, 6, 7))
ARRIVALS = tuple((m, q) for stage in ((2, 8, 1), (4, 3, 7), (5, 6)) for q in range(3) for m in stage)
HALF = BS // 2
KEPT = {0: 0, 2: 1, 6: 2}
ROUND = tuple(range(1, RING))


def kernel(
    factor, target, inverse, cols_in, pairs_in, out,
    left, own_0, own_1, slab, mate_0, mate_1, cols, pairs, mate_pairs, part, far, inv_out, inv_in, near, goal, kept, turned,
    local_sem, win_send, win_recv, end_send, mate_send, mate_recv, list_send, list_recv,
    sum_send, sum_recv, inv_send, inv_recv, greet,
):
    own, mate = (own_0, own_1), (mate_0, mate_1)
    group = lax.axis_index("rows")
    slot = lax.axis_index("inner")
    ring_at = slot // 2
    core = slot % 2
    other = slot + 1 - 2 * core
    first_row = group * 2 - BAND
    my_slice = pl.ds(pl.multiple_of(ring_at * SLICE, SLICE), SLICE)

    def along(step):
        return (group + step, slot)

    def around(step):
        return (group, lax.rem(ring_at + step + RING, RING) * 2 + core)

    sibling = (group, other)

    loads = [
        pltpu.make_async_copy(factor.at[:, slot, pl.ds(0, HALF)], own_0.at[0], local_sem.at[0]),
        pltpu.make_async_copy(factor.at[:, slot, pl.ds(HALF, HALF)], own_1.at[0], local_sem.at[1]),
        pltpu.make_async_copy(inverse.at[:, my_slice], slab.at[0], local_sem.at[2]),
        pltpu.make_async_copy(pairs_in, pairs, local_sem.at[3]),
        pltpu.make_async_copy(cols_in, cols, local_sem.at[4]),
        pltpu.make_async_copy(factor.at[:, other, pl.ds(0, HALF)], mate_0.at[0], local_sem.at[5]),
        pltpu.make_async_copy(factor.at[:, other, pl.ds(HALF, HALF)], mate_1.at[0], local_sem.at[6]),
        pltpu.make_async_copy(target, goal, local_sem.at[7]),
        pltpu.make_async_copy(factor, left, local_sem.at[8]),
    ]

    def remote(source, destination, send_sem, recv_sem, device):
        return pltpu.make_async_remote_copy(
            src_ref=source, dst_ref=destination, send_sem=send_sem, recv_sem=recv_sem,
            device_id=device, device_id_type=MESH,
        )

    def active(k, m):
        reach = 8 if k > m else m
        return jnp.logical_and(group >= k, group - k + reach < GROUPS)

    steps = {}
    for k, m in WINDOW:
        d = m - k
        sends = active(k, m)
        comes = jnp.logical_and(group >= m, group - m + (8 if k > m else m) < GROUPS)
        if d in steps:
            sends = jnp.logical_or(sends, steps[d][0])
            comes = jnp.logical_or(comes, steps[d][1])
        steps[d] = (sends, comes)
    for g, k, m in ENDS:
        d = m - k
        sends, comes = group == g + k, group == g + m
        if d in steps:
            sends = jnp.logical_or(sends, steps[d][0])
            comes = jnp.logical_or(comes, steps[d][1])
        steps[d] = (sends, comes)

    barrier = pltpu.get_barrier_semaphore()
    for step in (1, -1):
        pl.semaphore_signal(barrier, inc=1, device_id=around(step), device_id_type=MESH)
    pl.semaphore_signal(barrier, inc=1, device_id=sibling, device_id_type=MESH)
    partners = jnp.int32(3)
    for d, (sends, comes) in steps.items():
        @pl.when(comes)
        def _():
            pl.semaphore_signal(barrier, inc=1, device_id=along(-d), device_id_type=MESH)
        partners = partners + sends.astype(jnp.int32)
    for load in loads:
        load.start()
    for load in loads[:3]:
        load.wait()
    pl.semaphore_wait(barrier, partners)

    def piece(k, q):
        return slab.at[k] if q == 2 else own[q].at[k]

    def window_copy(k, m, q, send_sem):
        return remote(piece(k, q), piece(m, q), send_sem, win_recv.at[m - 1, q], along(m - k))

    def mate_copy(k, q):
        return remote(own[q].at[k], mate[q].at[k], mate_send.at[k - 1, q], mate_recv.at[k - 1, q], sibling)

    def pass_on(held, q):
        for n, (k, m) in enumerate(WINDOW):
            if k == held:
                @pl.when(active(k, m))
                def _():
                    window_copy(k, m, q, win_send.at[n, q]).start()
        for n, (g, k, m) in enumerate(ENDS):
            if k == held:
                @pl.when(group == g + k)
                def _():
                    window_copy(k, m, q, end_send.at[n, q]).start()
        if held and q < 2:
            mate_copy(held, q).start()

    list_copy = remote(pairs, mate_pairs, list_send.at[0], list_recv.at[0], sibling)

    def greeting(n):
        for way, step in enumerate((1, -1)):
            pl.semaphore_signal(greet.at[n, way], inc=1, device_id=around(step), device_id_type=MESH)

    def greeted(n):
        for way in range(2):
            pl.semaphore_wait(greet.at[n, way], 1)

    for q in range(3):
        pass_on(0, q)
    greeting(0)
    loads[3].wait()
    list_copy.start()

    def arrive(m, q):
        @pl.when(group >= m)
        def _():
            window_copy(0, m, q, win_send.at[0, q]).wait_recv()
            pass_on(m, q)

    def mates(q):
        for m in range(1, HOPS + 1):
            @pl.when(group >= m)
            def _():
                mate_copy(m, q).wait_recv()

    pending = list(ARRIVALS)

    def gather(upto):
        while pending:
            m, q = pending.pop(0)
            arrive(m, q)
            if (m, q) == upto:
                return

    for n in range(3):
        gather(ARRIVALS[3 * n + 2])
        greeted(n)
        if n < 2:
            greeting(n + 1)

    def locate(row, column):
        relative = cols[row, column] - first_row
        back = HOPS - lax.shift_right_arithmetic(relative, 1)
        return jnp.clip(back, 0, HOPS), relative & 1

    def partial_sums(e, q):
        column = lax.rem(ring_at + e, RING) * 2 + core
        totals = [jnp.zeros((HALF, BS), jnp.float32) for _ in range(2)]
        for table, window in ((pairs, own), (mate_pairs, mate)):
            for s in range(2):
                row = table[0, 0, 0, s, column]
                a = table[1, 0, 0, s, column]
                live = table[2, 0, 0, s, column]
                back, half = locate(row, column)
                product = lax.dot_general(
                    window[q][back, half], left[row, a],
                    (((1,), (1,)), ((), ())), preferred_element_type=jnp.float32,
                )
                for i in range(2):
                    wanted = jnp.logical_and(live == 1, row == i)
                    totals[i] = totals[i] + jnp.where(wanted, product, 0.0)
        return totals

    sent = []

    def hold(e, q):
        for i, total in enumerate(partial_sums(e, q)):
            part[q, e, i] = total.astype(jnp.bfloat16)

    def keep(e, q):
        for i, total in enumerate(partial_sums(e, q)):
            kept[q, KEPT[e], i] = total

    def sum_copy(n, q):
        source, destination, step = {
            0: (part.at[q, 3], near.at[q, 0], 1),
            1: (part.at[q, 5], near.at[q, 1], -1),
            2: (part.at[q, 4, 0], far.at[q, 0], -2),
            3: (part.at[q, 4, 1], far.at[q, 1], 2),
            4: (part.at[q, 1], near.at[q, 2], 1),
            5: (part.at[q, 7], near.at[q, 3], -1),
            6: (part.at[q, 2], near.at[q, 4], 2),
            7: (part.at[q, 6], near.at[q, 5], -2),
        }[n]
        return remote(source, destination, sum_send.at[n, q], sum_recv.at[n, q], around(step))

    def inverse_copy(e, place):
        return remote(inv_out.at[e], inv_in.at[:, place], inv_send.at[e - 1], inv_recv.at[e - 1], around(e))

    def send(copy):
        copy.start()
        sent.append(copy)

    def first_sums(q):
        hold(4, q)
        send(sum_copy(2, q))
        send(sum_copy(3, q))
        hold(3, q)
        send(sum_copy(0, q))
        hold(5, q)
        send(sum_copy(1, q))
        hold(1, q)
        send(sum_copy(4, q))
        hold(7, q)
        send(sum_copy(5, q))
        for e in (2, 6, 0):
            keep(e, q)

    def second_sums(q):
        for e, n, first, second, extra in ((2, 6, 0, 3, 1), (6, 7, 1, 2, 0)):
            sum_copy(first, q).wait_recv()
            sum_copy(second, q).wait_recv()
            for i in range(2):
                total = kept[q, KEPT[e], i] + near[q, first, i].astype(jnp.float32)
                if i == extra:
                    total = total + far[q, extra].astype(jnp.float32)
                part[q, e, i] = total.astype(jnp.bfloat16)
            send(sum_copy(n, q))

    def last_sums(q):
        totals = [kept[q, 0, i] for i in range(2)]
        for n in (4, 5, 6, 7):
            sum_copy(n, q).wait_recv()
            for i in range(2):
                totals[i] = totals[i] + near[q, n - 2, i].astype(jnp.float32)
        results = []
        for i in range(2):
            rows = pl.ds(q * HALF, HALF)
            difference = (turned[i, rows] - totals[i]).astype(jnp.bfloat16)
            results.append(lax.dot_general(
                difference, inv_in[i, rows], (((0,), (0,)), ((), ())), preferred_element_type=jnp.float32
            ))
        return results

    gather((6, 0))
    for load in loads[4:]:
        load.wait()
    list_copy.wait_recv()
    for i in range(2):
        turned[i] = goal[i, 0].astype(jnp.float32).T
    mates(0)
    first_sums(0)
    gather((6, 1))
    mates(1)
    first_sums(1)
    gather(None)
    for e in (4, 3, 5, 2, 6, 1, 7, 0):
        column = lax.rem(ring_at + e, RING) * 2 + core
        for i in range(2):
            back, half = locate(i, column)
            inv_out[e, i] = slab[back, half]
        if e:
            send(inverse_copy(e, my_slice))
    inv_in[:, my_slice, :] = inv_out[0]
    for q in range(2):
        second_sums(q)
    for e in ROUND:
        start = lax.rem(ring_at - e + RING, RING) * SLICE
        inverse_copy(e, pl.ds(pl.multiple_of(start, SLICE), SLICE)).wait_recv()
    lower = last_sums(0)
    upper = last_sums(1)
    for i in range(2):
        result = jnp.where(cols[i, slot] < 0, 0.0, lower[i] + upper[i])
        out[i, 0] = result.astype(jnp.bfloat16)
    for copy in sent:
        copy.wait_send()
    list_copy.wait_send()
    for q in range(3):
        for n, (k, m) in enumerate(WINDOW):
            @pl.when(active(k, m))
            def _():
                window_copy(k, m, q, win_send.at[n, q]).wait_send()
        for n, (g, k, m) in enumerate(ENDS):
            @pl.when(group == g + k)
            def _():
                window_copy(k, m, q, end_send.at[n, q]).wait_send()
        if q < 2:
            for m in range(1, HOPS + 1):
                @pl.when(group >= m)
                def _():
                    mate_copy(m, q).wait_send()


def per_device(factor, target_blocks, diag_inverse, cols, pair_list):
    bf16 = jnp.bfloat16
    anywhere = pl.BlockSpec(memory_space=pltpu.HBM)
    dma = pltpu.SemaphoreType.DMA
    return pl.pallas_call(
        kernel,
        out_shape=jax.ShapeDtypeStruct((2, 1, BS, BS), bf16),
        in_specs=[anywhere] * 5,
        out_specs=pl.BlockSpec(memory_space=pltpu.VMEM),
        scratch_shapes=[
            pltpu.VMEM((2, 16, BS, BS), bf16),
            pltpu.VMEM((HOPS + 1, 2, HALF, BS), bf16),
            pltpu.VMEM((HOPS + 1, 2, HALF, BS), bf16),
            pltpu.VMEM((HOPS + 1, 2, SLICE, BS), bf16),
            pltpu.VMEM((HOPS + 1, 2, HALF, BS), bf16),
            pltpu.VMEM((HOPS + 1, 2, HALF, BS), bf16),
            pltpu.SMEM((2, 16), jnp.int32),
            pltpu.SMEM((3, 1, 1, 2, 16), jnp.int32),
            pltpu.SMEM((3, 1, 1, 2, 16), jnp.int32),
            pltpu.VMEM((2, RING, 2, HALF, BS), bf16),
            pltpu.VMEM((2, 2, HALF, BS), bf16),
            pltpu.VMEM((RING, 2, SLICE, BS), bf16),
            pltpu.VMEM((2, BS, BS), bf16),
            pltpu.VMEM((2, 6, 2, HALF, BS), bf16),
            pltpu.VMEM((2, 1, BS, BS), bf16),
            pltpu.VMEM((2, 3, 2, HALF, BS), jnp.float32),
            pltpu.VMEM((2, BS, BS), jnp.float32),
            dma((9,)),
            dma((len(WINDOW), 3)),
            dma((HOPS, 3)),
            dma((len(ENDS), 3)),
            dma((HOPS, 2)),
            dma((HOPS, 2)),
            dma((1,)),
            dma((1,)),
            dma((8, 2)),
            dma((8, 2)),
            dma((RING - 1,)),
            dma((RING - 1,)),
            pltpu.SemaphoreType.REGULAR((3, 2)),
        ],
        compiler_params=pltpu.CompilerParams(
            collective_id=0, has_side_effects=True, vmem_limit_bytes=60 * 1024 * 1024
        ),
        name="sweep",
    )(factor, target_blocks, diag_inverse, cols, jnp.swapaxes(pair_list, 3, 4))


def solution(mesh):
    placed = (
        P("rows", None, None, None),
        P("rows", "inner", None, None),
        P("rows", None, None),
        P("rows", None),
        P(None, "rows", "inner", None, None),
    )
    return jax.shard_map(
        per_device,
        mesh=mesh,
        in_specs=placed,
        out_specs=P("rows", "inner", None, None),
        check_vma=False,
    )
```

time: 50.4 us -> 46.5 us (0.923)
  Pallas kernels: 48.7 us -> 44.8 us
    pallas_call x1, Pallas kernels: 48.7 us -> 44.8 us  [per_device(): pl.pallas_call(kernel, out_shape=jax.ShapeDtypeStruct((2, 1, BS, BS), bf1...]
where the time goes in v3:
time: 46.5 us; the launch traced here: 46.3 us
  Pallas kernels  44.8 us (96%)
  local copies, waits for them, and re-layouts  1.47 us (3%)
    pallas_call x1, Pallas kernels, per_device(): pl.pallas_call(kernel, out_shape=jax.ShapeDtypeStruct((2, 1, BS, BS), bf1...  44.8 us
    unnamed x1, local copies, waits for them, and re-layouts  1.47 us

profile of v3, /device:TPU:6, one launch (start us, length us, event | category | flops | bytes accessed | tf_op | source)
XLA Modules:
  0.0 46.3 jit_solution(2308300975907833092)
XLA Ops:
  0.0 44.8 %sweep.1 = bf16[2,1,128,128]{3,2,1,0:T(8,128)(2,1)} custom-call(bf16[2,16,128,128]{3,2,1,0:T(8,128)(2,1)} %factor.1, bf16[2,1,128,128]{3,2,1,0:T(8,128)(2,1)} %target.1, bf16[2,128,128]{2,1,0:T(8,128)(2,1)} %inverse.1, s32[2,16]{1,0:T(2,128)} %cols_in.1, s32[3,1,1,2,16]{4,3,2,1,0:T(2,128)} %bitcast.1), custom_call_target="tpu_custom_call" | custom-call | tf_op jit(solution)/shard_map/sweep/pallas_call | solution.py:314
  44.8 1.5 %copy.7 = bf16[2,1,128,128]{3,2,1,0:T(8,128)(2,1)} copy(bf16[2,1,128,128]{3,2,1,0:T(8,128)(2,1)} %sweep.1) | data formatting | bytes 131072

commit v4 on v3

--- a/solution.py
+++ b/solution.py
@@ -12,9 +12,9 @@
 RING = 8
 HOPS = 8
 SLICE = 16
-WINDOW = ((0, 2), (0, 8), (0, 1), (2, 4), (2, 3), (8, 7), (4, 5), (7, 6))
-ENDS = ((40, 4, 6), (41, 4, 6), (40, 6, 7))
-ARRIVALS = tuple((m, q) for stage in ((2, 8, 1), (4, 3, 7), (5, 6)) for q in range(3) for m in stage)
+WINDOW = ((0, 2), (0, 8), (2, 5), (2, 4), (2, 3), (2, 1), (8, 6), (8, 7))
+ENDS = ((40, 5, 7), (40, 5, 6), (41, 5, 6), (46, 0, 1))
+ARRIVALS = tuple((m, q) for stage in ((2, 8), (1, 3, 7, 4, 5, 6)) for q in range(3) for m in stage)
 HALF = BS // 2
 KEPT = {0: 0, 2: 1, 6: 2}
 ROUND = tuple(range(1, RING))
@@ -62,14 +62,13 @@
         )
 
     def active(k, m):
-        reach = 8 if k > m else m
-        return jnp.logical_and(group >= k, group - k + reach < GROUPS)
+        return jnp.logical_and(group >= k, group - k + max(k, m) < GROUPS)
 
     steps = {}
     for k, m in WINDOW:
         d = m - k
         sends = active(k, m)
-        comes = jnp.logical_and(group >= m, group - m + (8 if k > m else m) < GROUPS)
+        comes = jnp.logical_and(group >= m, group - m + max(k, m) < GROUPS)
         if d in steps:
             sends = jnp.logical_or(sends, steps[d][0])
             comes = jnp.logical_or(comes, steps[d][1])
@@ -270,7 +269,8 @@
     mates(1)
     first_sums(1)
     gather(None)
-    for e in (4, 3, 5, 2, 6, 1, 7, 0):
+    second_sums(0)
+    for e in (4, 3, 5, 0):
         column = lax.rem(ring_at + e, RING) * 2 + core
         for i in range(2):
             back, half = locate(i, column)
@@ -278,18 +278,6 @@
         if e:
             send(inverse_copy(e, my_slice))
     inv_in[:, my_slice, :] = inv_out[0]
-    for q in range(2):
-        second_sums(q)
-    for e in ROUND:
-        start = lax.rem(ring_at - e + RING, RING) * SLICE
-        inverse_copy(e, pl.ds(pl.multiple_of(start, SLICE), SLICE)).wait_recv()
-    lower = last_sums(0)
-    upper = last_sums(1)
-    for i in range(2):
-        result = jnp.where(cols[i, slot] < 0, 0.0, lower[i] + upper[i])
-        out[i, 0] = result.astype(jnp.bfloat16)
-    for copy in sent:
-        copy.wait_send()
     list_copy.wait_send()
     for q in range(3):
         for n, (k, m) in enumerate(WINDOW):
@@ -305,6 +293,28 @@
                 @pl.when(group >= m)
                 def _():
                     mate_copy(m, q).wait_send()
+    second_sums(1)
+    for e in (2, 6, 1, 7):
+        column = lax.rem(ring_at + e, RING) * 2 + core
+        for i in range(2):
+            back, half = locate(i, column)
+            inv_out[e, i] = slab[back, half]
+        if e:
+            send(inverse_copy(e, my_slice))
+    for e in ROUND:
+        start = lax.rem(ring_at - e + RING, RING) * SLICE
+        inverse_copy(e, pl.ds(pl.multiple_of(start, SLICE), SLICE)).wait_recv()
+    last = sent[-6:]
+    for copy in sent[:-6]:
+        copy.wait_send()
+    lower = last_sums(0)
+    upper = last_sums(1)
+    for i in range(2):
+        result = jnp.where(cols[i, slot] < 0, 0.0, lower[i] + upper[i])
+        out[i, 0] = result.astype(jnp.bfloat16)
+
+    for copy in last:
+        copy.wait_send()
 
 
 def per_device(factor, target_blocks, diag_inverse, cols, pair_list):

time: 46.5 us -> 44.9 us (0.966); the launches traced: 46.3 us -> 44.1 us
  Pallas kernels: 44.8 us -> 42.6 us
    pallas_call x1, Pallas kernels: 44.8 us -> 42.6 us  [per_device(): pl.pallas_call(kernel, out_shape=jax.ShapeDtypeStruct((2, 1, BS, BS), bf1...]
where the time goes in v4:
time: 44.9 us; the launch traced here: 44.1 us
  Pallas kernels  42.6 us (95%)
  local copies, waits for them, and re-layouts  1.47 us (3%)
    pallas_call x1, Pallas kernels, per_device(): pl.pallas_call(kernel, out_shape=jax.ShapeDtypeStruct((2, 1, BS, BS), bf1...  42.6 us
    unnamed x1, local copies, waits for them, and re-layouts  1.47 us

profile of v4, /device:TPU:6, one launch (start us, length us, event | category | flops | bytes accessed | tf_op | source)
XLA Modules:
  0.0 44.1 jit_solution(5178764494471972043)
XLA Ops:
  0.0 42.6 %sweep.1 = bf16[2,1,128,128]{3,2,1,0:T(8,128)(2,1)} custom-call(bf16[2,16,128,128]{3,2,1,0:T(8,128)(2,1)} %factor.1, bf16[2,1,128,128]{3,2,1,0:T(8,128)(2,1)} %target.1, bf16[2,128,128]{2,1,0:T(8,128)(2,1)} %inverse.1, s32[2,16]{1,0:T(2,128)} %cols_in.1, s32[3,1,1,2,16]{4,3,2,1,0:T(2,128)} %bitcast.1), custom_call_target="tpu_custom_call" | custom-call | tf_op jit(solution)/shard_map/sweep/pallas_call | solution.py:324
  42.6 1.5 %copy.7 = bf16[2,1,128,128]{3,2,1,0:T(8,128)(2,1)} copy(bf16[2,1,128,128]{3,2,1,0:T(8,128)(2,1)} %sweep.1) | data formatting | bytes 131072

commit v5 on v4

--- a/solution.py
+++ b/solution.py
@@ -36,7 +36,7 @@
     my_slice = pl.ds(pl.multiple_of(ring_at * SLICE, SLICE), SLICE)
 
     def along(step):
-        return (group + step, slot)
+        return (lax.rem(group + step + GROUPS, GROUPS), slot)
 
     def around(step):
         return (group, lax.rem(ring_at + step + RING, RING) * 2 + core)

time: 44.9 us -> 45 us (level)
  the two profiles are of different devices: /device:TPU:6 before, /device:TPU:19 now
where the time goes in v5:
time: 45 us; the launch traced here: 44.8 us
  Pallas kernels  43.3 us (96%)
  local copies, waits for them, and re-layouts  1.47 us (3%)
    pallas_call x1, Pallas kernels, per_device(): pl.pallas_call(kernel, out_shape=jax.ShapeDtypeStruct((2, 1, BS, BS), bf1...  43.3 us
    unnamed x1, local copies, waits for them, and re-layouts  1.47 us

profile of v5, /device:TPU:19, one launch (start us, length us, event | category | flops | bytes accessed | tf_op | source)
XLA Modules:
  0.0 44.8 jit_solution(18143055289269133152)
XLA Ops:
  0.0 43.3 %sweep.1 = bf16[2,1,128,128]{3,2,1,0:T(8,128)(2,1)} custom-call(bf16[2,16,128,128]{3,2,1,0:T(8,128)(2,1)} %factor.1, bf16[2,1,128,128]{3,2,1,0:T(8,128)(2,1)} %target.1, bf16[2,128,128]{2,1,0:T(8,128)(2,1)} %inverse.1, s32[2,16]{1,0:T(2,128)} %cols_in.1, s32[3,1,1,2,16]{4,3,2,1,0:T(2,128)} %bitcast.1), custom_call_target="tpu_custom_call" | custom-call | tf_op jit(solution)/shard_map/sweep/pallas_call | solution.py:324
  43.3 1.5 %copy.7 = bf16[2,1,128,128]{3,2,1,0:T(8,128)(2,1)} copy(bf16[2,1,128,128]{3,2,1,0:T(8,128)(2,1)} %sweep.1) | data formatting | bytes 131072

commit v6 on v5

--- a/solution.py
+++ b/solution.py
@@ -98,13 +98,14 @@
     pl.semaphore_wait(barrier, partners)
 
     def piece(k, q):
-        return slab.at[k] if q == 2 else own[q].at[k]
+        return slab.at[k, core] if q == 2 else own[q].at[k]
 
     def window_copy(k, m, q, send_sem):
         return remote(piece(k, q), piece(m, q), send_sem, win_recv.at[m - 1, q], along(m - k))
 
     def mate_copy(k, q):
-        return remote(own[q].at[k], mate[q].at[k], mate_send.at[k - 1, q], mate_recv.at[k - 1, q], sibling)
+        landing = piece(k, q) if q == 2 else mate[q].at[k]
+        return remote(piece(k, q), landing, mate_send.at[k - 1, q], mate_recv.at[k - 1, q], sibling)
 
     def pass_on(held, q):
         for n, (k, m) in enumerate(WINDOW):
@@ -117,7 +118,7 @@
                 @pl.when(group == g + k)
                 def _():
                     window_copy(k, m, q, end_send.at[n, q]).start()
-        if held and q < 2:
+        if held:
             mate_copy(held, q).start()
 
     list_copy = remote(pairs, mate_pairs, list_send.at[0], list_recv.at[0], sibling)
@@ -270,6 +271,7 @@
     first_sums(1)
     gather(None)
     second_sums(0)
+    mates(2)
     for e in (4, 3, 5, 0):
         column = lax.rem(ring_at + e, RING) * 2 + core
         for i in range(2):
@@ -288,11 +290,10 @@
             @pl.when(group == g + k)
             def _():
                 window_copy(k, m, q, end_send.at[n, q]).wait_send()
-        if q < 2:
-            for m in range(1, HOPS + 1):
-                @pl.when(group >= m)
-                def _():
-                    mate_copy(m, q).wait_send()
+        for m in range(1, HOPS + 1):
+            @pl.when(group >= m)
+            def _():
+                mate_copy(m, q).wait_send()
     second_sums(1)
     for e in (2, 6, 1, 7):
         column = lax.rem(ring_at + e, RING) * 2 + core
@@ -348,8 +349,8 @@
             dma((len(WINDOW), 3)),
             dma((HOPS, 3)),
             dma((len(ENDS), 3)),
-            dma((HOPS, 2)),
-            dma((HOPS, 2)),
+            dma((HOPS, 3)),
+            dma((HOPS, 3)),
             dma((1,)),
             dma((1,)),
             dma((8, 2)),

time: 45 us -> 44.7 us (level)
  the two profiles are of different devices: /device:TPU:19 before, /device:TPU:6 now
where the time goes in v6:
time: 44.7 us; the launch traced here: 44.1 us
  Pallas kernels  42.6 us (95%)
  local copies, waits for them, and re-layouts  1.47 us (3%)
    pallas_call x1, Pallas kernels, per_device(): pl.pallas_call(kernel, out_shape=jax.ShapeDtypeStruct((2, 1, BS, BS), bf1...  42.6 us
    unnamed x1, local copies, waits for them, and re-layouts  1.47 us

profile of v6, /device:TPU:6, one launch (start us, length us, event | category | flops | bytes accessed | tf_op | source)
XLA Modules:
  0.0 44.1 jit_solution(7556192834399617971)
XLA Ops:
  0.0 42.6 %sweep.1 = bf16[2,1,128,128]{3,2,1,0:T(8,128)(2,1)} custom-call(bf16[2,16,128,128]{3,2,1,0:T(8,128)(2,1)} %factor.1, bf16[2,1,128,128]{3,2,1,0:T(8,128)(2,1)} %target.1, bf16[2,128,128]{2,1,0:T(8,128)(2,1)} %inverse.1, s32[2,16]{1,0:T(2,128)} %cols_in.1, s32[3,1,1,2,16]{4,3,2,1,0:T(2,128)} %bitcast.1), custom_call_target="tpu_custom_call" | custom-call | tf_op jit(solution)/shard_map/sweep/pallas_call | solution.py:325
  42.6 1.5 %copy.7 = bf16[2,1,128,128]{3,2,1,0:T(8,128)(2,1)} copy(bf16[2,1,128,128]{3,2,1,0:T(8,128)(2,1)} %sweep.1) | data formatting | bytes 131072
